TPU v7x, 32 devices: a whole 2x2x4 slice. The times are simulated.
32 devices in a mesh: req: 16 (over z, x, core), tp: 2 (over y).
Axes of the slice: x: 2, y: 2, z: 4, core: 2. Of those that a mesh axis runs over, the one named last changes fastest.
Arguments:
- suffix_query: bfloat16 [4096, 5120], P('req', 'tp')
- suffix_key: bfloat16 [4096, 1024], P('req', 'tp')
- suffix_value: bfloat16 [4096, 1024], P('req', 'tp'), may hold values from -6 to 6
- prefix_key: bfloat16 [16, 1024, 1024], P('req', None, 'tp')
- prefix_value: bfloat16 [16, 1024, 1024], P('req', None, 'tp'), may hold values from -6 to 6
- residual: bfloat16 [4096, 5120], P('req'), may hold values from -6 to 6
- out_weight: bfloat16 [5120, 5120], P('tp'), may hold values from -0.15625 to 0.15625
- norm_gain: bfloat16 [5120], P('tp'), may hold values from 0.099609375 to 1.8984375
- lengths: int32 [16], replicated, may hold values from 1 to 256, 2457 in all
- request_slot: int32 [16], replicated, may hold values from 0 to 15, each once
- prefix_owner: int32 [16], replicated, may hold values from 0 to 15, each once
- request_group: int32 [16, 1], replicated, may hold values from 0 to 3
Outputs:
- hidden: bfloat16 [4096, 5120], P('req', 'tp')
- normed: bfloat16 [4096, 5120], P('req', 'tp')
- cache_key: bfloat16 [4096, 1024], P('req', 'tp')
Inputs may be any that keep to these rules, and one draw needn't show every extreme that they name: `request_slot`: a permutation. `prefix_owner`: a permutation. `request_group`: every group has one request or more. `lengths`: some request has all 256 slots live.
All inputs are finite; a program needn't handle non-finite values.
Results may differ from a plain program's by a relative error of at most 0.0067.
Values may be sent and summed in bfloat16 or wider, within the bound.
A program may use at most 128 MiB of HBM per device.

v0:
```python
import jax
import jax.numpy as jnp
from jax import lax
from jax.sharding import PartitionSpec as P

HD = 128
GROUPS = 4


THETA = 1000000.0
NEGATIVE = -1e30
EPSILON = 1e-06


def rotate(values, head_count, position_base):
    row_count = values.shape[0]
    half_dim = HD // 2
    positions = (position_base + jnp.arange(row_count)).astype(jnp.float32)
    frequency = THETA ** (-(jnp.arange(half_dim).astype(jnp.float32) * 2.0 / HD))
    angles = positions[:, None] * frequency[None, :]
    cosines = jnp.cos(angles)[:, None, :]
    sines = jnp.sin(angles)[:, None, :]
    per_head = values.reshape(row_count, head_count, HD)
    front_half = per_head[..., :half_dim]
    back_half = per_head[..., half_dim:]
    joined = jnp.concatenate(
        [front_half * cosines - back_half * sines, back_half * cosines + front_half * sines],
        axis=-1,
    )
    return joined.reshape(row_count, head_count * HD)


def attend(queries, keys_in, values_in, visible):
    row_count = queries.shape[0]
    kv_count = keys_in.shape[-1] // HD
    ratio = queries.shape[1] // HD // kv_count
    query_heads = queries.reshape(row_count, kv_count, ratio, HD)
    key_heads = keys_in.reshape(-1, kv_count, HD)
    value_heads = values_in.reshape(-1, kv_count, HD)
    scores = jnp.einsum(
        "sgrd,kgd->sgrk", query_heads, key_heads, preferred_element_type=jnp.float32
    ) * HD ** (-0.5)
    if visible is not None:
        scores = jnp.where(visible[:, None, None, :], scores, NEGATIVE)
    block_max = jnp.max(scores, axis=-1)
    weights = jnp.exp(scores - block_max[..., None])
    block_sum = jnp.sum(weights, axis=-1)
    probs = weights.astype(jnp.bfloat16)
    block_out = (
        jnp.einsum("sgrk,kgd->sgrd", probs, value_heads, preferred_element_type=jnp.float32)
        / block_sum[..., None]
    )
    heads = kv_count * ratio
    return (
        block_max.reshape(row_count, heads),
        block_sum.reshape(row_count, heads),
        block_out.reshape(row_count, heads, HD),
    )


def absorb(state, incoming):
    running_max, running_sum, running_out = state
    part_max, part_sum, part_out = incoming
    new_max = jnp.maximum(running_max, part_max)
    keep_scale = jnp.exp(running_max - new_max)
    fresh_weight = part_sum * jnp.exp(part_max - new_max)
    return (
        new_max,
        running_sum * keep_scale + fresh_weight,
        running_out * keep_scale[..., None] + fresh_weight[..., None] * part_out,
    )


def lookup(table, numbers, wanted):
    return jnp.sum(jnp.where(numbers == wanted, table, 0))


def shards(
    suffix_query,
    suffix_key,
    suffix_value,
    prefix_key,
    prefix_value,
    residual,
    out_weight,
    norm_gain,
    lengths,
    request_slot,
    prefix_owner,
    request_group,
):
    slots = suffix_query.shape[0]
    query_heads = suffix_query.shape[1] // HD
    kv_heads = suffix_key.shape[1] // HD
    devices = lax.axis_size("req")
    place = lax.axis_index("req")
    per_group = devices // GROUPS
    prefix_length = prefix_key.shape[1] * per_group
    numbers = jnp.arange(devices, dtype=jnp.int32)
    owner_match = prefix_owner[None, :] == numbers[:, None]
    holder_group = jnp.sum(jnp.where(owner_match, numbers[None, :], 0), axis=1) // per_group
    slot_match = request_slot[:, None] == numbers[None, :]
    asker_group = jnp.sum(jnp.where(slot_match, request_group[:, 0][None, :], 0), axis=1)
    asker_length = jnp.sum(jnp.where(slot_match, lengths[None, :], 0), axis=1)
    group_here = lookup(asker_group, numbers, place)
    length_here = lookup(asker_length, numbers, place)
    positions = jnp.arange(slots, dtype=jnp.int32)
    queries = rotate(suffix_query.astype(jnp.float32), query_heads, prefix_length).astype(
        jnp.bfloat16
    )
    keys_rot = rotate(suffix_key.astype(jnp.float32), kv_heads, prefix_length)
    live_rows = positions < length_here
    cache_key = jnp.where(live_rows[:, None], keys_rot, 0.0).astype(jnp.bfloat16)
    visible = (positions[None, :] <= positions[:, None]) & (positions[None, :] < length_here)
    own_max, own_sum, own_out = attend(queries, cache_key, suffix_value, visible)
    state = (own_max, own_sum, own_sum[..., None] * own_out)
    key_blocks = lax.all_gather(prefix_key, "req", axis=0, tiled=True)
    value_blocks = lax.all_gather(prefix_value, "req", axis=0, tiled=True)
    block_count = key_blocks.shape[0]

    def visit(inner, entry):
        key_block, value_block, device = entry
        wanted = lookup(holder_group, numbers, device) == group_here

        def include(current):
            part_max, part_sum, part_out = attend(queries, key_block, value_block, None)
            rounded = lax.optimization_barrier(part_out.astype(jnp.bfloat16)).astype(jnp.float32)
            return absorb(current, (part_max, part_sum, rounded))

        def passing(current):
            return current

        return (lax.cond(wanted, include, passing, inner), None)

    devices_here = jnp.arange(block_count, dtype=jnp.int32)
    result, _ = lax.scan(visit, state, (key_blocks, value_blocks, devices_here))
    running_max, running_sum, running_out = result
    mixed = jnp.where(live_rows[:, None, None], running_out / running_sum[..., None], 0.0)
    attn = mixed.astype(jnp.bfloat16).reshape(slots, query_heads * HD)
    projected = jnp.dot(attn, out_weight, preferred_element_type=jnp.float32)
    width_total = residual.shape[1]
    columns = width_total // lax.axis_size("tp")
    column_start = lax.axis_index("tp") * columns
    shared_part = lax.psum_scatter(projected, "tp", scatter_dimension=1, tiled=True)
    own_residual = lax.dynamic_slice_in_dim(residual, column_start, columns, 1)
    hidden = (own_residual.astype(jnp.float32) + shared_part).astype(jnp.bfloat16)
    widened = hidden.astype(jnp.float32)
    row_squares = lax.psum(jnp.sum(widened * widened, axis=1), "tp")
    scale_rows = lax.rsqrt(row_squares / width_total + EPSILON)
    normed = (widened * scale_rows[:, None] * norm_gain.astype(jnp.float32)[None, :]).astype(
        jnp.bfloat16
    )
    return (hidden, normed, cache_key)


def solution(mesh):
    return jax.shard_map(
        shards,
        mesh=mesh,
        in_specs=(
            P("req", "tp"),
            P("req", "tp"),
            P("req", "tp"),
            P("req", None, "tp"),
            P("req", None, "tp"),
            P("req", None),
            P("tp", None),
            P("tp"),
            P(),
            P(),
            P(),
            P(),
        ),
        out_specs=(P("req", "tp"), P("req", "tp"), P("req", "tp")),
        check_vma=False,
    )
```

profile of v0, /device:TPU:0, one launch (start us, length us, event | category | flops | bytes accessed | tf_op | source)
XLA Modules:
  0.0 576.4 jit_solution(9660801580665399996)
XLA Ops:
  14.2 3.4 fusion.14
  17.6 3.7 fusion.13
  22.2 4.1 bitcast_divide_fusion.1
  27.3 112.5 %all-gather.3.cloned.1.call-done = bf16[16,1024,512]{2,1,0:T(8,128)(2,1)} async-done(((bf16[1,1024,512]{2,1,0:T(8,128)(2,1)}), bf16[16,1024,512]{2,1,0:T(8,128)(2,1)}) %all-gather.3.cloned.1.call-update) | async-done | bytes 16777232 | tf_op jit(solution)/shard_map/all_gather | solution.py:117
  139.8 21.8 %copy.69 = bf16[16,1024,512]{1,2,0:T(8,128)(2,1)} copy(bf16[16,1024,512]{2,1,0:T(8,128)(2,1)} %all-gather.3.cloned.1.call-done) | data formatting | bytes 33554432
  161.7 105.4 %all-gather.5.cloned.1.call-done = bf16[16,1024,512]{2,1,0:T(8,128)(2,1)} async-done(((bf16[1,1024,512]{2,1,0:T(8,128)(2,1)}), bf16[16,1024,512]{2,1,0:T(8,128)(2,1)}) %all-gather.5.cloned.1.call-update) | async-done | bytes 16777232 | tf_op jit(solution)/shard_map/all_gather | solution.py:118
  267.1 21.6 %copy.70 = bf16[16,1024,512]{1,2,0:T(8,128)(2,1)} copy(bf16[16,1024,512]{2,1,0:T(8,128)(2,1)} %all-gather.5.cloned.1.call-done) | data formatting | bytes 33554432
  288.7 189.5 %while.16 = (s32[]{:T(128)}, f32[256,20]{0,1:T(8,128)S(1)}, f32[256,20]{0,1:T(8,128)S(1)}, f32[256,20,128]{2,0,1:T(8,128)S(1)}, s32[16]{0:T(128)S(1)}, /*index=5...) while((s32[]{:T(128)}, f32[256,20]{0,1:T(8,128)S(1)}, ...), condition=%wide.region_13.14_spmd.clone, body=%wide.region_7.13_spmd.clone.sunk | while | flops 2730250240 | bytes 88207816 | solution.py:136
  289.3 1.3 fusion.51
  291.9 34.5 %conditional.3 = ((f32[256,20]{0,1:T(8,128)S(1)}, f32[256,20]{0,1:T(8,128)S(1)}, f32[256,20,128]{2,0,1:T(8,128)S(1)})) conditional(s32[]{:T(128)} %convert_element_type.153, (f32[256,20]{0,1:T(8,128)S(1)}, f32[256,20]{0,1:T(8,128)S(1)}, f32[256,20,128]{2,0,1:T(8,128)S(1)}) %tuple.58, (bf16[16,1024,512]{1,2,0:T(8,128)(2,1)}, s32[]{:T(128)}, ...), branch_computations={%region_9.9_spmd, %region_10.12_spmd} | conditional | flops 2730250240 | bytes 88207456 | solution.py:133
  291.9 2.8 constant_dynamic-slice_fusion
  294.7 8.5 %bitcast_reduce_fusion = (f32[256,4,5]{0,2,1:T(8,128)S(1)}, f32[4,1024,256,5]{2,1,3,0:T(8,128)}) fusion(bf16[1024,4,128,1]{0,2,3,1:T(8,128)(2,1)S(1)} %bitcast.82, bf16[256,4,5,128]{0,3,2,1:T(8,128)(2,1)S(1)} %bitcast.85), kind=kOutput, calls=%fused_computation.1 | convolution fusion | flops 1352657920 | bytes 23351296 | tf_op jit(solution)/shard_map/while/body/eval_jaxpr/cond/branch_1_fun/sgrd,kgd->sgrk/dot_general | solution.py:40
  303.3 9.1 %fusion.2 = f32[256,4,5]{0,2,1:T(8,128)S(1)} fusion(f32[4,1024,256,5]{2,1,3,0:T(8,128)} %get-tuple-element.232, f32[256,4,5]{0,2,1:T(8,128)S(1)} %get-tuple-element.231), kind=kLoop, calls=%fused_computation.4 | loop fusion | flops 15723520 | bytes 21012480 | tf_op jit(solution)/shard_map/while/body/eval_jaxpr/cond/branch_1_fun/reduce_sum | solution.py:47
  312.3 10.6 %fusion.7 = bf16[256,4,5,128]{3,0,2,1:T(8,128)(2,1)} fusion(bf16[1024,4,128,1]{0,2,3,1:T(8,128)(2,1)S(1)} %bitcast.87, f32[4,1024,256,5]{2,1,3,0:T(8,128)} %get-tuple-element.232, f32[256,4,5]{0,2,1:T(8,128)S(1)} %get-tuple-element.231, f32[256,4,5]{0,2,1:T(8,128)S(1)} %fusion.2), kind=kOutput, calls=%fused_computation.9 | convolution fusion | flops 1359216640 | bytes 23371776 | tf_op jit(solution)/shard_map/while/body/eval_jaxpr/cond/branch_1_fun/sgrk,kgd->sgrd/dot_general | solution.py:50
  323.0 3.4 multiply_add_fusion
  327.0 1.3 fusion.51
  330.2 1.3 fusion.51
  333.4 1.3 fusion.51
  336.7 1.3 fusion.51
  339.9 1.3 fusion.51
  343.2 1.3 fusion.51
  345.8 34.5 %conditional.3 = ((f32[256,20]{0,1:T(8,128)S(1)}, f32[256,20]{0,1:T(8,128)S(1)}, f32[256,20,128]{2,0,1:T(8,128)S(1)})) conditional(s32[]{:T(128)} %convert_element_type.153, (f32[256,20]{0,1:T(8,128)S(1)}, f32[256,20]{0,1:T(8,128)S(1)}, f32[256,20,128]{2,0,1:T(8,128)S(1)}) %tuple.58, (bf16[16,1024,512]{1,2,0:T(8,128)(2,1)}, s32[]{:T(128)}, ...), branch_computations={%region_9.9_spmd, %region_10.12_spmd} | conditional | flops 2730250240 | bytes 88207456 | solution.py:133
  345.8 2.8 constant_dynamic-slice_fusion
  348.6 8.5 %bitcast_reduce_fusion = (f32[256,4,5]{0,2,1:T(8,128)S(1)}, f32[4,1024,256,5]{2,1,3,0:T(8,128)}) fusion(bf16[1024,4,128,1]{0,2,3,1:T(8,128)(2,1)S(1)} %bitcast.82, bf16[256,4,5,128]{0,3,2,1:T(8,128)(2,1)S(1)} %bitcast.85), kind=kOutput, calls=%fused_computation.1 | convolution fusion | flops 1352657920 | bytes 23351296 | tf_op jit(solution)/shard_map/while/body/eval_jaxpr/cond/branch_1_fun/sgrd,kgd->sgrk/dot_general | solution.py:40
  357.1 9.1 %fusion.2 = f32[256,4,5]{0,2,1:T(8,128)S(1)} fusion(f32[4,1024,256,5]{2,1,3,0:T(8,128)} %get-tuple-element.232, f32[256,4,5]{0,2,1:T(8,128)S(1)} %get-tuple-element.231), kind=kLoop, calls=%fused_computation.4 | loop fusion | flops 15723520 | bytes 21012480 | tf_op jit(solution)/shard_map/while/body/eval_jaxpr/cond/branch_1_fun/reduce_sum | solution.py:47
  366.2 10.6 %fusion.7 = bf16[256,4,5,128]{3,0,2,1:T(8,128)(2,1)} fusion(bf16[1024,4,128,1]{0,2,3,1:T(8,128)(2,1)S(1)} %bitcast.87, f32[4,1024,256,5]{2,1,3,0:T(8,128)} %get-tuple-element.232, f32[256,4,5]{0,2,1:T(8,128)S(1)} %get-tuple-element.231, f32[256,4,5]{0,2,1:T(8,128)S(1)} %fusion.2), kind=kOutput, calls=%fused_computation.9 | convolution fusion | flops 1359216640 | bytes 23371776 | tf_op jit(solution)/shard_map/while/body/eval_jaxpr/cond/branch_1_fun/sgrk,kgd->sgrd/dot_general | solution.py:50
  376.9 3.4 multiply_add_fusion
  380.8 1.3 fusion.51
  383.4 34.5 %conditional.3 = ((f32[256,20]{0,1:T(8,128)S(1)}, f32[256,20]{0,1:T(8,128)S(1)}, f32[256,20,128]{2,0,1:T(8,128)S(1)})) conditional(s32[]{:T(128)} %convert_element_type.153, (f32[256,20]{0,1:T(8,128)S(1)}, f32[256,20]{0,1:T(8,128)S(1)}, f32[256,20,128]{2,0,1:T(8,128)S(1)}) %tuple.58, (bf16[16,1024,512]{1,2,0:T(8,128)(2,1)}, s32[]{:T(128)}, ...), branch_computations={%region_9.9_spmd, %region_10.12_spmd} | conditional | flops 2730250240 | bytes 88207456 | solution.py:133
  383.5 2.8 constant_dynamic-slice_fusion
  386.3 8.5 %bitcast_reduce_fusion = (f32[256,4,5]{0,2,1:T(8,128)S(1)}, f32[4,1024,256,5]{2,1,3,0:T(8,128)}) fusion(bf16[1024,4,128,1]{0,2,3,1:T(8,128)(2,1)S(1)} %bitcast.82, bf16[256,4,5,128]{0,3,2,1:T(8,128)(2,1)S(1)} %bitcast.85), kind=kOutput, calls=%fused_computation.1 | convolution fusion | flops 1352657920 | bytes 23351296 | tf_op jit(solution)/shard_map/while/body/eval_jaxpr/cond/branch_1_fun/sgrd,kgd->sgrk/dot_general | solution.py:40
  394.8 9.1 %fusion.2 = f32[256,4,5]{0,2,1:T(8,128)S(1)} fusion(f32[4,1024,256,5]{2,1,3,0:T(8,128)} %get-tuple-element.232, f32[256,4,5]{0,2,1:T(8,128)S(1)} %get-tuple-element.231), kind=kLoop, calls=%fused_computation.4 | loop fusion | flops 15723520 | bytes 21012480 | tf_op jit(solution)/shard_map/while/body/eval_jaxpr/cond/branch_1_fun/reduce_sum | solution.py:47
  403.9 10.6 %fusion.7 = bf16[256,4,5,128]{3,0,2,1:T(8,128)(2,1)} fusion(bf16[1024,4,128,1]{0,2,3,1:T(8,128)(2,1)S(1)} %bitcast.87, f32[4,1024,256,5]{2,1,3,0:T(8,128)} %get-tuple-element.232, f32[256,4,5]{0,2,1:T(8,128)S(1)} %get-tuple-element.231, f32[256,4,5]{0,2,1:T(8,128)S(1)} %fusion.2), kind=kOutput, calls=%fused_computation.9 | convolution fusion | flops 1359216640 | bytes 23371776 | tf_op jit(solution)/shard_map/while/body/eval_jaxpr/cond/branch_1_fun/sgrk,kgd->sgrd/dot_general | solution.py:50
  414.5 3.4 multiply_add_fusion
  418.5 1.3 fusion.51
  437.3 34.5 %conditional.3 = ((f32[256,20]{0,1:T(8,128)S(1)}, f32[256,20]{0,1:T(8,128)S(1)}, f32[256,20,128]{2,0,1:T(8,128)S(1)})) conditional(s32[]{:T(128)} %convert_element_type.153, (f32[256,20]{0,1:T(8,128)S(1)}, f32[256,20]{0,1:T(8,128)S(1)}, f32[256,20,128]{2,0,1:T(8,128)S(1)}) %tuple.58, (bf16[16,1024,512]{1,2,0:T(8,128)(2,1)}, s32[]{:T(128)}, ...), branch_computations={%region_9.9_spmd, %region_10.12_spmd} | conditional | flops 2730250240 | bytes 88207456 | solution.py:133
  437.3 2.8 constant_dynamic-slice_fusion
  440.1 8.5 %bitcast_reduce_fusion = (f32[256,4,5]{0,2,1:T(8,128)S(1)}, f32[4,1024,256,5]{2,1,3,0:T(8,128)}) fusion(bf16[1024,4,128,1]{0,2,3,1:T(8,128)(2,1)S(1)} %bitcast.82, bf16[256,4,5,128]{0,3,2,1:T(8,128)(2,1)S(1)} %bitcast.85), kind=kOutput, calls=%fused_computation.1 | convolution fusion | flops 1352657920 | bytes 23351296 | tf_op jit(solution)/shard_map/while/body/eval_jaxpr/cond/branch_1_fun/sgrd,kgd->sgrk/dot_general | solution.py:40
  448.7 9.1 %fusion.2 = f32[256,4,5]{0,2,1:T(8,128)S(1)} fusion(f32[4,1024,256,5]{2,1,3,0:T(8,128)} %get-tuple-element.232, f32[256,4,5]{0,2,1:T(8,128)S(1)} %get-tuple-element.231), kind=kLoop, calls=%fused_computation.4 | loop fusion | flops 15723520 | bytes 21012480 | tf_op jit(solution)/shard_map/while/body/eval_jaxpr/cond/branch_1_fun/reduce_sum | solution.py:47
  457.7 10.6 %fusion.7 = bf16[256,4,5,128]{3,0,2,1:T(8,128)(2,1)} fusion(bf16[1024,4,128,1]{0,2,3,1:T(8,128)(2,1)S(1)} %bitcast.87, f32[4,1024,256,5]{2,1,3,0:T(8,128)} %get-tuple-element.232, f32[256,4,5]{0,2,1:T(8,128)S(1)} %get-tuple-element.231, f32[256,4,5]{0,2,1:T(8,128)S(1)} %fusion.2), kind=kOutput, calls=%fused_computation.9 | convolution fusion | flops 1359216640 | bytes 23371776 | tf_op jit(solution)/shard_map/while/body/eval_jaxpr/cond/branch_1_fun/sgrk,kgd->sgrd/dot_general | solution.py:50
  468.4 3.4 multiply_add_fusion
  478.2 2.1 copy.71
  480.3 2.0 select_convert_fusion
  482.4 14.4 %fusion.42 = f32[256,5120]{1,0:T(8,128)} fusion(bf16[256,2560]{0,1:T(8,128)(2,1)S(1)} %bitcast.88, bf16[2560,5120]{1,0:T(8,128)(2,1)} %param.22), kind=kOutput, calls=%fused_computation.79 | convolution fusion | flops 6710886400 | bytes 32768000 | tf_op jit(solution)/shard_map/dot_general | solution.py:140
  498.8 62.1 %reduce-scatter.2.cloned.1.call-done = f32[256,2560]{1,0:T(8,128)} async-done(((f32[256,5120]{1,0:T(8,128)}), f32[256,2560]{1,0:T(8,128)}) %reduce-scatter.2.cloned.1.call-update) | async-done | bytes 2621456 | tf_op jit(solution)/shard_map/reduce_scatter | solution.py:144
  560.9 2.6 fusion.15
  563.5 4.9 psum.7
  568.4 1.4 fusion.17
  (125 shorter events, 29.7 us)
Async XLA Ops:
  7.2 2.1 copy-start.10
  7.2 2.9 copy-start.9
  7.2 3.0 copy-start.8
  7.2 132.6 %all-gather.3.cloned.1.call-start = ((), (), s32[]{:S(2)}) async-start(), calls=%async_computation.1 | async-start | bytes 17825792 | tf_op jit(solution)/shard_map/all_gather | solution.py:117
  7.9 259.1 %all-gather.5.cloned.1.call-start = ((), (), s32[]{:S(2)}) async-start(), calls=%async_computation.2 | async-start | bytes 17825792 | tf_op jit(solution)/shard_map/all_gather | solution.py:118
  8.7 552.2 %reduce-scatter.2.cloned.1.call-start = ((), (), s32[]{:S(2)}) async-start(), calls=%async_computation.3 | async-start | bytes 7864320 | tf_op jit(solution)/shard_map/reduce_scatter | solution.py:144
  10.8 0.7 copy-start.13
  10.9 0.7 copy-start.14
  10.9 0.7 copy-start.15
  13.6 4.0 copy-start
  14.2 3.4 copy-start.4
  14.2 3.4 copy-start.6
  17.6 3.8 copy-start.16
  17.6 4.6 copy-start.11
  291.9 2.8 copy-start.1
  303.3 9.1 %copy-start.2 = (bf16[1,1024,512]{1,2,0:T(8,128)(2,1)S(1)}, bf16[1,1024,512]{1,2,0:T(8,128)(2,1)}, u32[]{:S(2)}) copy-start(bf16[1,1024,512]{1,2,0:T(8,128)(2,1)} %get-tuple-element.233) | copy-start | bytes 3145732 | tf_op jit(solution)/shard_map/while/body/eval_jaxpr/cond
  345.8 2.8 copy-start.1
  357.1 9.1 %copy-start.2 = (bf16[1,1024,512]{1,2,0:T(8,128)(2,1)S(1)}, bf16[1,1024,512]{1,2,0:T(8,128)(2,1)}, u32[]{:S(2)}) copy-start(bf16[1,1024,512]{1,2,0:T(8,128)(2,1)} %get-tuple-element.233) | copy-start | bytes 3145732 | tf_op jit(solution)/shard_map/while/body/eval_jaxpr/cond
  383.5 2.8 copy-start.1
  394.8 9.1 %copy-start.2 = (bf16[1,1024,512]{1,2,0:T(8,128)(2,1)S(1)}, bf16[1,1024,512]{1,2,0:T(8,128)(2,1)}, u32[]{:S(2)}) copy-start(bf16[1,1024,512]{1,2,0:T(8,128)(2,1)} %get-tuple-element.233) | copy-start | bytes 3145732 | tf_op jit(solution)/shard_map/while/body/eval_jaxpr/cond
  437.3 2.8 copy-start.1
  448.6 9.1 %copy-start.2 = (bf16[1,1024,512]{1,2,0:T(8,128)(2,1)S(1)}, bf16[1,1024,512]{1,2,0:T(8,128)(2,1)}, u32[]{:S(2)}) copy-start(bf16[1,1024,512]{1,2,0:T(8,128)(2,1)} %get-tuple-element.233) | copy-start | bytes 3145732 | tf_op jit(solution)/shard_map/while/body/eval_jaxpr/cond
  496.8 0.7 copy-start.12
  496.8 1.0 copy-start.5
  496.8 1.0 copy-start.7
  563.5 6.4 %copy-start.3 = (bf16[256,2560]{1,0:T(8,128)(2,1)}, bf16[256,2560]{1,0:T(8,128)(2,1)S(1)}, u32[]{:S(2)}) copy-start(bf16[256,2560]{1,0:T(8,128)(2,1)S(1)} %get-tuple-element.230) | copy-start | bytes 3932164
Sparse Core Ops, SparseCore 0:
  10.2 129.5 all-gather.2
  142.0 125.0 all-gather.4
  497.0 63.8 reduce-scatter.1
where the time goes:
time: 578 us; the launch traced here: 576 us
  waiting for transfers between devices  281 us (49%)
  matrix products  98.5 us (17%)
  other arithmetic  86.6 us (15%)
  local copies, waits for them, and re-layouts  69.7 us (12%)
  loops' own time  21.1 us (4%)
  between operations  14 us (2%)
    all_gather x1, waiting for transfers between devices, shards(): key_blocks = lax.all_gather(prefix_key, 'req', axis=0, tiled=True)  113 us
    all_gather x1, waiting for transfers between devices, shards(): value_blocks = lax.all_gather(prefix_value, 'req', axis=0, tiled=True)  105 us
    reduce_scatter x1, waiting for transfers between devices, shards(): lax.psum_scatter(projected, 'tp', scatter_dimension=1, tiled=True)  62.1 us
    dot_general x5, matrix products, attend(): jnp.einsum('sgrk,kgd->sgrd', probs, value_heads, preferred_element_type=j...  46.6 us
    unnamed x33, local copies, waits for them, and re-layouts  45.5 us
    reduce_sum x5, other arithmetic, attend(): block_sum = jnp.sum(weights, axis=-1)  39.9 us
    dot_general x5, matrix products, attend(): jnp.einsum('sgrd,kgd->sgrk', query_heads, key_heads, preferred_element_ty...  37.5 us
    reduce_sum x17, other arithmetic, lookup(): return jnp.sum(jnp.where(numbers == wanted, table, 0))  22.1 us
  transfers between devices with their start and end apart: 3, of which 3 were waited for; matrix products, arithmetic and copies ran while one was open for 7% of the time, Pallas kernels for 0%

commit v1 on v0

v1 whole, which is shorter than its diff:
```python
import functools

import jax
import jax.numpy as jnp
from jax import lax
from jax.experimental import pallas as pl
from jax.experimental.pallas import tpu as pltpu
from jax.sharding import PartitionSpec as P

HD = 128
GROUPS = 4

THETA = 1000000.0
NEGATIVE = -1e30
EPSILON = 1e-06
LOG2E = 1.4426950408889634


def rope_tables(row_count, position_base):
    half_dim = HD // 2
    positions = (position_base + jnp.arange(row_count)).astype(jnp.float32)
    frequency = THETA ** (-(jnp.arange(half_dim).astype(jnp.float32) * 2.0 / HD))
    angles = positions[:, None] * frequency[None, :]
    cosines, sines = jnp.cos(angles), jnp.sin(angles)
    return (
        jnp.concatenate([cosines, cosines], axis=1),
        jnp.concatenate([-sines, sines], axis=1),
    )


def attention_kernel(
    per_group, ratio, numbers, query, key, value, cosines, sines, block, out, rotated, top, total, acc
):
    step = pl.program_id(0)
    scale = HD**-0.5 * LOG2E
    length = numbers[per_group]
    slots = query.shape[0]
    across = (((1,), (1,)), ((), ()))

    @pl.when(step == 0)
    def _():
        rows = lax.broadcasted_iota(jnp.int32, (slots, slots), 0)
        cols = lax.broadcasted_iota(jnp.int32, (slots, slots), 1)
        visible = (cols <= rows) & (cols < length)
        for r in range(ratio):
            head = query[:, r * HD : (r + 1) * HD].astype(jnp.float32)
            turned = pltpu.roll(head, HD // 2, 1)
            q = (head * cosines[...] + turned * sines[...]).astype(jnp.bfloat16)
            rotated[r] = q
            s = lax.dot_general(q, key[...], across, preferred_element_type=jnp.float32)
            s = jnp.where(visible, s, NEGATIVE)
            m = jnp.max(s, axis=1, keepdims=True)
            p = jnp.exp2((s - m) * scale)
            top[r] = jnp.broadcast_to(m, (slots, HD))
            total[r] = jnp.broadcast_to(jnp.sum(p, axis=1, keepdims=True), (slots, HD))
            acc[r] = jnp.dot(
                p.astype(jnp.bfloat16), value[...], preferred_element_type=jnp.float32
            )

    keys = block[0, :, :HD]
    values = block[0, :, HD:]
    for r in range(ratio):
        s = lax.dot_general(rotated[r], keys, across, preferred_element_type=jnp.float32)
        before = top[r][:, :1]
        m = jnp.maximum(before, jnp.max(s, axis=1, keepdims=True))
        keep = jnp.exp2((before - m) * scale)
        p = jnp.exp2((s - m) * scale)
        top[r] = jnp.broadcast_to(m, (slots, HD))
        total[r] = total[r] * keep + jnp.sum(p, axis=1, keepdims=True)
        acc[r] = acc[r] * keep + jnp.dot(
            p.astype(jnp.bfloat16), values, preferred_element_type=jnp.float32
        )

    @pl.when(step == per_group - 1)
    def _():
        live = lax.broadcasted_iota(jnp.int32, (slots, HD), 0) < length
        for r in range(ratio):
            o = jnp.where(live, acc[r] / total[r], 0.0)
            out[:, r * HD : (r + 1) * HD] = o.astype(jnp.bfloat16)


def attention(head, numbers, query, key, value, cosines, sines, gathered, ratio):
    slots = query.shape[0]
    per_group = numbers.shape[0] - 1
    pblk = gathered.shape[1]
    width = ratio * HD
    fixed = lambda j: (lambda b, n: (0, j))
    return pl.pallas_call(
        functools.partial(attention_kernel, per_group, ratio),
        out_shape=jax.ShapeDtypeStruct((slots, width), jnp.bfloat16),
        grid_spec=pltpu.PrefetchScalarGridSpec(
            num_scalar_prefetch=1,
            grid=(per_group,),
            in_specs=[
                pl.BlockSpec((slots, width), fixed(head)),
                pl.BlockSpec((slots, HD), fixed(head)),
                pl.BlockSpec((slots, HD), fixed(head)),
                pl.BlockSpec((slots, HD), fixed(0)),
                pl.BlockSpec((slots, HD), fixed(0)),
                pl.BlockSpec((1, pblk, 2 * HD), lambda b, n: (n[b], 0, 0)),
            ],
            out_specs=pl.BlockSpec((slots, width), fixed(0)),
            scratch_shapes=[
                pltpu.VMEM((ratio, slots, HD), jnp.bfloat16),
                pltpu.VMEM((ratio, slots, HD), jnp.float32),
                pltpu.VMEM((ratio, slots, HD), jnp.float32),
                pltpu.VMEM((ratio, slots, HD), jnp.float32),
            ],
        ),
        compiler_params=pltpu.CompilerParams(vmem_limit_bytes=32 * 1024 * 1024),
        cost_estimate=pl.CostEstimate(
            flops=4 * slots * width * pblk * per_group * 4,
            bytes_accessed=per_group * pblk * 2 * HD * 2 + 2 * slots * width * 2,
            transcendentals=slots * ratio * pblk * per_group,
        ),
    )(numbers, query, key, value, cosines, sines, gathered)


def shards(
    suffix_query,
    suffix_key,
    suffix_value,
    prefix_key,
    prefix_value,
    residual,
    out_weight,
    norm_gain,
    lengths,
    request_slot,
    prefix_owner,
    request_group,
):
    slots = suffix_query.shape[0]
    kv_heads = suffix_key.shape[1] // HD
    ratio = suffix_query.shape[1] // HD // kv_heads
    devices = lax.axis_size("req")
    sides = lax.axis_size("tp")
    side = lax.axis_index("tp")
    per_group = devices // GROUPS
    prefix_length = prefix_key.shape[1] * per_group
    width_total = residual.shape[1]
    columns = width_total // sides
    chunk = ratio * HD
    first_last = (kv_heads - 1) * chunk

    def send(array, shift):
        return lax.ppermute(array, "tp", [(i, (i + shift) % sides) for i in range(sides)])

    def columns_of(array, shift):
        start = lax.rem(side + shift, sides) * columns
        return lax.dynamic_slice_in_dim(array, start, columns, 1)

    gathered = []
    for head in range(kv_heads):
        cut = slice(head * HD, (head + 1) * HD)
        both = jnp.concatenate([prefix_key[:, :, cut], prefix_value[:, :, cut]], axis=2)
        if gathered:
            both, gathered[-1] = lax.optimization_barrier((both, gathered[-1]))
        gathered.append(lax.all_gather(both, "req", axis=0, tiled=True))

    last_rows = out_weight[first_last:]
    weights_in = [send(columns_of(last_rows, shift), shift) for shift in range(1, sides)]

    request = request_slot[lax.axis_index("req")]
    group_here = request_group[request, 0]
    length_here = lengths[request]
    holders = lax.dynamic_slice_in_dim(prefix_owner, group_here * per_group, per_group)
    numbers = jnp.concatenate([holders, length_here[None]]).astype(jnp.int32)

    cosines, sines = rope_tables(slots, prefix_length)
    per_head = suffix_key.astype(jnp.float32).reshape(slots, kv_heads, HD)
    turned = jnp.concatenate([per_head[..., HD // 2 :], per_head[..., : HD // 2]], axis=-1)
    keys_rot = per_head * cosines[:, None, :] + turned * sines[:, None, :]
    live_rows = jnp.arange(slots, dtype=jnp.int32) < length_here
    cache_key = (
        jnp.where(live_rows[:, None, None], keys_rot, 0.0)
        .astype(jnp.bfloat16)
        .reshape(slots, kv_heads * HD)
    )

    attn = []
    for head in range(kv_heads):
        attn.append(
            attention(
                head, numbers, suffix_query, cache_key, suffix_value, cosines, sines,
                gathered[head], ratio,
            )
        )

    own = columns_of(residual, 0).astype(jnp.float32)
    projected = None
    for head in range(kv_heads - 1):
        term = jnp.dot(
            attn[head],
            out_weight[head * chunk : (head + 1) * chunk],
            preferred_element_type=jnp.float32,
        )
        projected = term if projected is None else projected + term
    if projected is not None:
        own = own + columns_of(projected, 0)
        for shift in range(1, sides):
            part = columns_of(projected, shift).astype(jnp.bfloat16)
            own = own + send(part, shift).astype(jnp.float32)
    last_in = [send(attn[-1], shift) for shift in range(1, sides)]
    own = own + jnp.dot(attn[-1], columns_of(last_rows, 0), preferred_element_type=jnp.float32)
    for last, weight in zip(last_in, weights_in):
        own = own + jnp.dot(last, weight, preferred_element_type=jnp.float32)

    hidden = own.astype(jnp.bfloat16)
    widened = hidden.astype(jnp.float32)
    mine = jnp.sum(widened * widened, axis=1)
    row_squares = mine
    for shift in range(1, sides):
        row_squares = row_squares + send(mine, shift)
    scale_rows = lax.rsqrt(row_squares / width_total + EPSILON)
    normed = (widened * scale_rows[:, None] * norm_gain.astype(jnp.float32)[None, :]).astype(
        jnp.bfloat16
    )
    return (hidden, normed, cache_key)


def solution(mesh):
    return jax.shard_map(
        shards,
        mesh=mesh,
        in_specs=(
            P("req", "tp"),
            P("req", "tp"),
            P("req", "tp"),
            P("req", None, "tp"),
            P("req", None, "tp"),
            P("req", None),
            P("tp", None),
            P("tp"),
            P(),
            P(),
            P(),
            P(),
        ),
        out_specs=(P("req", "tp"), P("req", "tp"), P("req", "tp")),
        check_vma=False,
    )
```

time: 578 us -> 385 us (0.67)
  other arithmetic: 86.6 us -> 7.96 us
  matrix products: 98.5 us -> 23.1 us
  Pallas kernels: 0 us -> 58.2 us
  local copies, waits for them, and re-layouts: 69.7 us -> 27.7 us
  waiting for transfers between devices: 281 us -> 245 us
  loops' own time: 21.1 us -> 0 us
    dot_general x11 -> x5, matrix products: 98.5 us -> 23.1 us  [the longest x3 15.8 us: shards(): jnp.dot(attn[head], out_weight[head * chunk:(head + 1) * chunk], preferre...]
    reduce_sum x25 -> x0, other arithmetic: 64.9 us -> none  [the longest x5 39.9 us: attend(): block_sum = jnp.sum(weights, axis=-1)]
    reduce_scatter x1 -> x0, waiting for transfers between devices: 62.1 us -> none  [shards(): lax.psum_scatter(projected, 'tp', scatter_dimension=1, tiled=True)]
    pallas_call x0 -> x4, Pallas kernels: none -> 58.2 us  [attention(): pl.pallas_call(functools.partial(attention_kernel, per_group, ratio), out...]
    unnamed x33 -> x34, local copies, waits for them, and re-layouts: 45.5 us -> 12.9 us
    another operation x17 -> x0, loops' own time: 21.1 us -> none  [the longest x1 20.7 us: shards(): result, _ = lax.scan(visit, state, (key_blocks, value_blocks, devices_here))]
    ppermute x0 -> x4, waiting for transfers between devices: none -> 17.6 us  [send(): lax.ppermute(array, 'tp', [(i, (i + shift) % sides) for i in range(sides)])]
    dynamic_slice x20 -> x4, local copies, waits for them, and re-layouts: 20.5 us -> 5.26 us  [the longest x1 4.01 us: columns_of(): return lax.dynamic_slice_in_dim(array, start, columns, 1)]
  transfers between devices with their start and end apart: 3 -> 8, of which waited for: 3 -> 6; matrix products, arithmetic and copies ran while one was open for 7% -> 10% of each run, Pallas kernels for 0% -> 15%
where the time goes in v1:
time: 385 us
  waiting for transfers between devices  245 us (64%)
  Pallas kernels  58.2 us (15%)
  local copies, waits for them, and re-layouts  27.7 us (7%)
  matrix products  23.1 us (6%)
  between operations  17.9 us (5%)
  other arithmetic  7.96 us (2%)
  starting transfers between devices  4.34 us (1%)
    all_gather x4, waiting for transfers between devices, shards(): gathered.append(lax.all_gather(both, 'req', axis=0, tiled=True))  228 us
    pallas_call x4, Pallas kernels, attention(): pl.pallas_call(functools.partial(attention_kernel, per_group, ratio), out...  58.2 us
    ppermute x4, waiting for transfers between devices, send(): lax.ppermute(array, 'tp', [(i, (i + shift) % sides) for i in range(sides)])  17.6 us
    dot_general x3, matrix products, shards(): jnp.dot(attn[head], out_weight[head * chunk:(head + 1) * chunk], preferre...  15.8 us
    unnamed x34, local copies, waits for them, and re-layouts  12.9 us
  transfers between devices with their start and end apart: 8, of which 6 were waited for; matrix products, arithmetic and copies ran while one was open for 10% of the time, Pallas kernels for 15%

profile of v1, /device:TPU:0, one launch (start us, length us, event | category | flops | bytes accessed | tf_op | source)
XLA Modules:
  0.0 384.5 jit_solution(12441668962948395825)
XLA Ops:
  7.2 1.7 fusion.21
  8.9 0.9 pad_maximum_fusion.1
  9.8 0.0 all-gather.7.cloned.1.call-start
  9.9 0.9 pad_maximum_fusion
  10.7 77.7 %all-gather.5.cloned.1.call-done.block = bf16[16,1024,256]{2,1,0:T(8,128)(2,1)} async-done(((bf16[1,1024,256]{2,1,0:T(8,128)(2,1)}), bf16[16,1024,256]{2,1,0:T(8,128)(2,1)}) %all-gather.5.cloned.1.call-update) | async-done | bytes 8388624 | tf_op jit(solution)/shard_map/all_gather | solution.py:159
  88.4 0.0 all-gather.9.cloned.1.call-start
  88.4 0.9 pad_maximum_fusion.2
  89.3 75.0 %all-gather.7.cloned.1.call-done.block = bf16[16,1024,256]{2,1,0:T(8,128)(2,1)} async-done(((bf16[1,1024,256]{2,1,0:T(8,128)(2,1)}), bf16[16,1024,256]{2,1,0:T(8,128)(2,1)}) %all-gather.7.cloned.1.call-update) | async-done | bytes 8388624 | tf_op jit(solution)/shard_map/all_gather | solution.py:159
  164.3 0.9 pad_maximum_fusion.3
  165.2 75.0 %all-gather.9.cloned.1.call-done.block = bf16[16,1024,256]{2,1,0:T(8,128)(2,1)} async-done(((bf16[1,1024,256]{2,1,0:T(8,128)(2,1)}), bf16[16,1024,256]{2,1,0:T(8,128)(2,1)}) %all-gather.9.cloned.1.call-update) | async-done | bytes 8388624 | tf_op jit(solution)/shard_map/all_gather | solution.py:159
  240.2 6.0 %slice.55 = bf16[640,5120]{1,0:T(8,128)(2,1)} slice(bf16[2560,5120]{1,0:T(8,128)(2,1)} %param.18), slice={[1920:2560], [0:5120]} | slice | bytes 13107200 | tf_op jit(solution)/shard_map/slice | solution.py:161
  246.2 4.0 %constant_dynamic-slice_fusion = bf16[640,2560]{1,0:T(8,128)(2,1)} fusion(bf16[640,5120]{1,0:T(8,128)(2,1)} %slice.55, s32[]{:T(128)S(6)} %select_n.29), kind=kLoop, calls=%fused_computation.31 | loop fusion | bytes 6553604 | tf_op jit(solution)/shard_map/dynamic_slice | solution.py:151
  250.3 1.4 collective-permute-start.2
  251.7 0.6 dynamic_slice.28
  254.2 0.6 fusion.24
  256.1 0.6 dynamic_slice.31
  256.7 0.2 reshape.36
  257.5 0.1 dynamic_slice.30
  257.6 0.7 pad_add_fusion.numbers
  258.3 0.7 iota_compare_fusion
  259.0 0.5 multiply_cosine_fusion
  259.6 0.1 pad_maximum_fusion.4
  259.7 0.3 fusion.23
  260.1 0.4 maximum_multiply_fusion
  260.4 0.1 mul.97
  260.5 0.1 fusion.18.key
  260.6 0.2 copy-done.4
  260.9 3.4 copy-done.1
  264.3 14.4 %shard_map.139 = bf16[256,640]{1,0:T(8,128)(2,1)S(1)} custom-call(s32[5]{0:T(128)S(1)} %pad_add_fusion.numbers, bf16[256,2560]{1,0:T(8,128)(2,1)S(1)} %copy-done.4, bf16[256,512]{1,0:T(8,128)(2,1)S(1)} %fusion.18.key, bf16[256,512]{1,0:T(8,128)(2,1)S(1)} %copy-done.5, f32[256,128]{1,0:T(8,128)S(1)} %get-tuple-element.30.cosines, ...), custom_call_target="tpu_custom_call" | custom-call | flops 10737418240 | bytes 2752512 | tf_op jit(solution)/shard_map/pallas_call | solution.py:88
  278.7 5.3 %fusion.10 = f32[256,5120]{1,0:T(8,128)S(1)} fusion(bf16[256,640]{1,0:T(8,128)(2,1)S(1)} %shard_map.139, bf16[2560,5120]{1,0:T(8,128)(2,1)} %param.18), kind=kOutput, calls=%fused_computation.6 | convolution fusion | flops 1677721600 | bytes 12124160 | tf_op jit(solution)/shard_map/dot_general | solution.py:193
  284.1 3.4 copy-done.2
  287.5 14.5 %shard_map.140 = bf16[256,640]{1,0:T(8,128)(2,1)S(1)} custom-call(s32[5]{0:T(128)S(1)} %pad_add_fusion.numbers, bf16[256,2560]{1,0:T(8,128)(2,1)S(1)} %copy-done.4, bf16[256,512]{1,0:T(8,128)(2,1)S(1)} %fusion.18.key, bf16[256,512]{1,0:T(8,128)(2,1)S(1)} %copy-done.5, f32[256,128]{1,0:T(8,128)S(1)} %get-tuple-element.30.cosines, ...), custom_call_target="tpu_custom_call" | custom-call | flops 10737418240 | bytes 2752512 | tf_op jit(solution)/shard_map/pallas_call | solution.py:88
  302.0 5.3 %fusion.7 = f32[256,5120]{1,0:T(8,128)S(1)} fusion(f32[256,5120]{1,0:T(8,128)S(1)} %fusion.10, bf16[256,640]{1,0:T(8,128)(2,1)S(1)} %shard_map.140, bf16[2560,5120]{1,0:T(8,128)(2,1)} %param.18), kind=kOutput, calls=%fused_computation.5 | convolution fusion | flops 1679032320 | bytes 17367040 | tf_op jit(solution)/shard_map/dot_general | solution.py:193
  307.3 14.8 %shard_map.141 = bf16[256,640]{1,0:T(8,128)(2,1)S(1)} custom-call(s32[5]{0:T(128)S(1)} %pad_add_fusion.numbers, bf16[256,2560]{1,0:T(8,128)(2,1)S(1)} %copy-done.4, bf16[256,512]{1,0:T(8,128)(2,1)S(1)} %fusion.18.key, bf16[256,512]{1,0:T(8,128)(2,1)S(1)} %copy-done.5, f32[256,128]{1,0:T(8,128)S(1)} %get-tuple-element.30.cosines, ...), custom_call_target="tpu_custom_call" | custom-call | flops 10737418240 | bytes 2752512 | tf_op jit(solution)/shard_map/pallas_call | solution.py:88
  322.1 5.3 %fusion.2 = f32[256,5120]{1,0:T(8,128)S(1)} fusion(f32[256,5120]{1,0:T(8,128)S(1)} %fusion.7, bf16[256,640]{1,0:T(8,128)(2,1)S(1)} %shard_map.141, bf16[2560,5120]{1,0:T(8,128)(2,1)} %param.18), kind=kOutput, calls=%fused_computation.2 | convolution fusion | flops 1679032320 | bytes 17367040 | tf_op jit(solution)/shard_map/dot_general | solution.py:193
  327.4 2.4 copy-done.6
  329.8 1.2 dynamic-slice_convert_fusion
  331.0 0.6 collective-permute-start
  331.6 3.4 copy-done.3
  335.0 14.5 %shard_map.142 = bf16[256,640]{1,0:T(8,128)(2,1)S(1)} custom-call(s32[5]{0:T(128)S(1)} %pad_add_fusion.numbers, bf16[256,2560]{1,0:T(8,128)(2,1)S(1)} %copy-done.4, bf16[256,512]{1,0:T(8,128)(2,1)S(1)} %fusion.18.key, bf16[256,512]{1,0:T(8,128)(2,1)S(1)} %copy-done.5, f32[256,128]{1,0:T(8,128)S(1)} %get-tuple-element.30.cosines, ...), custom_call_target="tpu_custom_call" | custom-call | flops 10737418240 | bytes 2752512 | tf_op jit(solution)/shard_map/pallas_call | solution.py:88
  349.5 1.5 collective-permute-start.1
  351.0 3.3 fusion.12
  354.3 8.7 %collective-permute-done = bf16[256,2560]{1,0:T(8,128)(2,1)} collective-permute-done((bf16[256,2560]{1,0:T(8,128)(2,1)}, bf16[256,2560]{1,0:T(8,128)(2,1)}, u32[]{:S(2)}, u32[]{:S(2)}) %collective-permute-start) | collective-permute-done | bytes 1310752 | tf_op jit(solution)/shard_map/ppermute | solution.py:147
  363.0 5.9 %collective-permute-done.1 = bf16[256,640]{1,0:T(8,128)(2,1)S(1)} collective-permute-done((bf16[256,640]{1,0:T(8,128)(2,1)S(1)}, bf16[256,640]{1,0:T(8,128)(2,1)S(1)}, u32[]{:S(2)}, u32[]{:S(2)}) %collective-permute-start.1) | collective-permute-done | bytes 327712 | tf_op jit(solution)/shard_map/ppermute | solution.py:147
  368.9 4.0 %fusion.14 = (f32[256]{0:T(256)S(1)}, bf16[256,2560]{1,0:T(8,128)(2,1)S(1)}) fusion(f32[256,2560]{1,0:T(8,128)S(1)} %fusion.12, bf16[256,2560]{1,0:T(8,128)(2,1)} %collective-permute-done, f32[256,5120]{1,0:T(8,128)S(1)} %copy-done.7, s32[]{:T(128)S(6)} %select_n.24, bf16[256,5120]{1,0:T(8,128)(2,1)} %param.17, ...), kind=kOutput, calls=%fused_computation.12 | convolution fusion | flops 845414144 | bytes 12780548 | tf_op jit(solution)/shard_map/dot_general | solution.py:207
  372.9 0.7 collective-permute-start.3
  373.6 3.0 collective-permute-done.3
  376.5 1.4 fusion.16
  (42 shorter events, 0.3 us)
Async XLA Ops:
  7.2 81.2 %all-gather.5.cloned.1.call-start = ((), (), s32[]{:S(2)}) async-start(), calls=%async_computation | async-start | bytes 8912896 | tf_op jit(solution)/shard_map/all_gather | solution.py:159
  9.8 154.5 %all-gather.7.cloned.1.call-start = ((), (), s32[]{:S(2)}) async-start(), calls=%async_computation.1 | async-start | bytes 8912896 | tf_op jit(solution)/shard_map/all_gather | solution.py:159
  88.4 151.8 %all-gather.9.cloned.1.call-start = ((), (), s32[]{:S(2)}) async-start(), calls=%async_computation.2 | async-start | bytes 8912896 | tf_op jit(solution)/shard_map/all_gather | solution.py:159
  164.3 167.3 %all-gather.11.cloned.1.call-start = ((), (), s32[]{:S(2)}) async-start(), calls=%async_computation.3 | async-start | bytes 8912896 | tf_op jit(solution)/shard_map/all_gather | solution.py:159
  246.2 5.5 %copy-start.11 = (s32[16]{0:T(128)S(1)}, s32[16]{0:T(128)}, u32[]{:S(2)}) copy-start(s32[16]{0:T(128)} %param.21) | copy-start | bytes 196
  246.2 8.0 %copy-start.12 = (s32[16,1]{0,1:T(1,128)S(1)}, s32[16,1]{0,1:T(1,128)}, u32[]{:S(2)}) copy-start(s32[16,1]{0,1:T(1,128)} %param.23) | copy-start | bytes 196
  246.2 9.9 %copy-start.13 = (s32[16]{0:T(128)S(1)}, s32[16]{0:T(128)}, u32[]{:S(2)}) copy-start(s32[16]{0:T(128)} %param.20) | copy-start | bytes 196
  246.2 10.5 %copy-start.9 = (bf16[256,512]{1,0:T(8,128)(2,1)S(1)}, bf16[256,512]{1,0:T(8,128)(2,1)}, u32[]{:S(2)}) copy-start(bf16[256,512]{1,0:T(8,128)(2,1)} %param.13) | copy-start | bytes 786436
  246.2 11.3 %copy-start.14 = (s32[16]{0:T(128)S(1)}, s32[16]{0:T(128)}, u32[]{:S(2)}) copy-start(s32[16]{0:T(128)} %param.22) | copy-start | bytes 196
  250.3 104.0 %collective-permute-start.2 = (bf16[640,2560]{1,0:T(8,128)(2,1)}, bf16[640,2560]{1,0:T(8,128)(2,1)}, u32[]{:S(2)}, u32[]{:S(2)}) collective-permute-start(bf16[640,2560]{1,0:T(8,128)(2,1)} %constant_dynamic-slice_fusion), channel_id=1, source_target_pairs={{0,1},{1,0},{2,3},{3,2},{4,5},{5,4},{6,7},{7,6},{8,9},{9,8},{10,11... | collective-permute-start | bytes 9830408 | tf_op jit(solution)/shard_map/ppermute | solution.py:147
  259.6 1.3 copy-start.4
  259.6 1.3 copy-start.5
  260.9 3.4 copy-start.1
  264.3 67.3 %copy-start = (bf16[256,512]{1,0:T(8,128)(2,1)}, bf16[256,512]{1,0:T(8,128)(2,1)S(1)}, u32[]{:S(2)}) copy-start(bf16[256,512]{1,0:T(8,128)(2,1)S(1)} %fusion.18.key) | copy-start | bytes 786436
  278.7 28.6 %slice-start = ((s8[8388608]{0:T(1024)(128)(4,1)}), s8[4194304]{0:T(1024)(128)(4,1)S(1)}, s32[]{:S(2)}) async-start(s8[8388608]{0:T(1024)(128)(4,1)} %bitcast.21), calls=%async_computation.4 | async-start | bytes 8388608
  284.1 3.4 copy-start.2
  287.5 19.8 %slice-start.1 = ((s8[8388608]{0:T(1024)(128)(4,1)}), s8[4194304]{0:T(1024)(128)(4,1)S(1)}, s32[]{:S(2)}) async-start(s8[8388608]{0:T(1024)(128)(4,1)} %bitcast.21), calls=%async_computation.5 | async-start | bytes 8388608
  327.4 2.4 copy-start.6
  331.0 32.0 %collective-permute-start = (bf16[256,2560]{1,0:T(8,128)(2,1)}, bf16[256,2560]{1,0:T(8,128)(2,1)}, u32[]{:S(2)}, u32[]{:S(2)}) collective-permute-start(bf16[256,2560]{1,0:T(8,128)(2,1)} %dynamic-slice_convert_fusion), channel_id=1, source_target_pairs={{0,1},{1,0},{2,3},{3,2},{4,5},{5,4},{6,7},{7,6},{8,9},{9,8},{10,11... | collective-permute-start | bytes 3932168 | tf_op jit(solution)/shard_map/ppermute | solution.py:147
  331.6 3.4 copy-start.3
  349.5 19.4 %collective-permute-start.1 = (bf16[256,640]{1,0:T(8,128)(2,1)S(1)}, bf16[256,640]{1,0:T(8,128)(2,1)S(1)}, u32[]{:S(2)}, u32[]{:S(2)}) collective-permute-start(bf16[256,640]{1,0:T(8,128)(2,1)S(1)} %shard_map.142), channel_id=1, source_target_pairs={{0,1},{1,0},{2,3},{3,2},{4,5},{5,4},{6,7},{7,6},{8,9},{9,8},{10,11... | collective-permute-start | bytes 983048 | tf_op jit(solution)/shard_map/ppermute | solution.py:147
  351.0 17.9 %copy-start.7 = (f32[256,5120]{1,0:T(8,128)S(1)}, f32[256,5120]{1,0:T(8,128)}, u32[]{:S(2)}) copy-start(f32[256,5120]{1,0:T(8,128)} %copy-done.6) | copy-start | bytes 15728644
  354.2 19.3 %copy-start.10 = (bf16[2560]{0:T(1024)(128)(2,1)S(1)}, bf16[2560]{0:T(1024)(128)(2,1)}, u32[]{:S(2)}) copy-start(bf16[2560]{0:T(1024)(128)(2,1)} %param.19) | copy-start | bytes 15364
  372.9 5.1 %copy-start.8 = (bf16[256,2560]{1,0:T(8,128)(2,1)}, bf16[256,2560]{1,0:T(8,128)(2,1)S(1)}, u32[]{:S(2)}) copy-start(bf16[256,2560]{1,0:T(8,128)(2,1)S(1)} %get-tuple-element.16) | copy-start | bytes 3932164
  372.9 3.6 collective-permute-start.3
Sparse Core Ops, SparseCore 0:
  10.7 77.5 all-gather.4
  91.1 73.1 all-gather.6
  167.0 73.1 all-gather.8
  242.8 73.1 all-gather.10

commit v2 on v1

--- a/solution.py
+++ b/solution.py
@@ -79,7 +79,7 @@
             out[:, r * HD : (r + 1) * HD] = o.astype(jnp.bfloat16)
 
 
-def attention(head, numbers, query, key, value, cosines, sines, gathered, ratio):
+def attention(head, numbers, query, key, value, cosines, sines, gathered, place, ratio):
     slots = query.shape[0]
     per_group = numbers.shape[0] - 1
     pblk = gathered.shape[1]
@@ -97,7 +97,7 @@
                 pl.BlockSpec((slots, HD), fixed(head)),
                 pl.BlockSpec((slots, HD), fixed(0)),
                 pl.BlockSpec((slots, HD), fixed(0)),
-                pl.BlockSpec((1, pblk, 2 * HD), lambda b, n: (n[b], 0, 0)),
+                pl.BlockSpec((1, pblk, 2 * HD), lambda b, n: (n[b], 0, place)),
             ],
             out_specs=pl.BlockSpec((slots, width), fixed(0)),
             scratch_shapes=[
@@ -107,7 +107,7 @@
                 pltpu.VMEM((ratio, slots, HD), jnp.float32),
             ],
         ),
-        compiler_params=pltpu.CompilerParams(vmem_limit_bytes=32 * 1024 * 1024),
+        compiler_params=pltpu.CompilerParams(vmem_limit_bytes=56 * 1024 * 1024),
         cost_estimate=pl.CostEstimate(
             flops=4 * slots * width * pblk * per_group * 4,
             bytes_accessed=per_group * pblk * 2 * HD * 2 + 2 * slots * width * 2,
@@ -150,16 +150,13 @@
         start = lax.rem(side + shift, sides) * columns
         return lax.dynamic_slice_in_dim(array, start, columns, 1)
 
-    gathered = []
-    for head in range(kv_heads):
+    def last_columns(shift):
+        start = lax.rem(side + shift, sides) * columns
+        return lax.dynamic_slice(out_weight, (first_last, start), (chunk, columns))
+
+    def pair(head):
         cut = slice(head * HD, (head + 1) * HD)
-        both = jnp.concatenate([prefix_key[:, :, cut], prefix_value[:, :, cut]], axis=2)
-        if gathered:
-            both, gathered[-1] = lax.optimization_barrier((both, gathered[-1]))
-        gathered.append(lax.all_gather(both, "req", axis=0, tiled=True))
-
-    last_rows = out_weight[first_last:]
-    weights_in = [send(columns_of(last_rows, shift), shift) for shift in range(1, sides)]
+        return jnp.concatenate([prefix_key[:, :, cut], prefix_value[:, :, cut]], axis=2)
 
     request = request_slot[lax.axis_index("req")]
     group_here = request_group[request, 0]
@@ -178,12 +175,25 @@
         .reshape(slots, kv_heads * HD)
     )
 
+    last_out = [last_columns(shift) for shift in range(1, sides)]
+    last_pair = pair(kv_heads - 1)
+    sources = []
+    if kv_heads > 1:
+        first = jnp.concatenate([pair(head) for head in range(kv_heads - 1)], axis=2)
+        first = lax.all_gather(first, "req", axis=0, tiled=True)
+        first, last_pair, numbers, cache_key, cosines, sines, last_out = lax.optimization_barrier(
+            (first, last_pair, numbers, cache_key, cosines, sines, last_out)
+        )
+        sources = [(first, head) for head in range(kv_heads - 1)]
+    sources.append((lax.all_gather(last_pair, "req", axis=0, tiled=True), 0))
+    weights_in = [send(last_out[shift - 1], shift) for shift in range(1, sides)]
+
     attn = []
     for head in range(kv_heads):
         attn.append(
             attention(
                 head, numbers, suffix_query, cache_key, suffix_value, cosines, sines,
-                gathered[head], ratio,
+                *sources[head], ratio,
             )
         )
 
@@ -202,7 +212,7 @@
             part = columns_of(projected, shift).astype(jnp.bfloat16)
             own = own + send(part, shift).astype(jnp.float32)
     last_in = [send(attn[-1], shift) for shift in range(1, sides)]
-    own = own + jnp.dot(attn[-1], columns_of(last_rows, 0), preferred_element_type=jnp.float32)
+    own = own + jnp.dot(attn[-1], last_columns(0), preferred_element_type=jnp.float32)
     for last, weight in zip(last_in, weights_in):
         own = own + jnp.dot(last, weight, preferred_element_type=jnp.float32)
 

time: 385 us -> 271 us (0.70)
  waiting for transfers between devices: 245 us -> 137 us
  local copies, waits for them, and re-layouts: 27.7 us -> 15.1 us
  Pallas kernels: 58.2 us -> 65.2 us
    all_gather x4 -> x2, waiting for transfers between devices: 228 us -> 125 us  [the longest x1 118 us: shards(): first = lax.all_gather(first, 'req', axis=0, tiled=True)]
    pallas_call x4, Pallas kernels: 58.2 us -> 65.2 us  [attention(): pl.pallas_call(functools.partial(attention_kernel, per_group, ratio), out...]
    unnamed x34 -> x31, local copies, waits for them, and re-layouts: 12.9 us -> 6.66 us
    ppermute x4, waiting for transfers between devices: 17.6 us -> 11.7 us  [send(): lax.ppermute(array, 'tp', [(i, (i + shift) % sides) for i in range(sides)])]
    slice x2, local copies, waits for them, and re-layouts: 7.7 us -> 2.24 us  [the longest x1 1.12 us: pair(): prefix_key[:, :, cut]]
  transfers between devices with their start and end apart: 8 -> 6, of which waited for: 6 -> 5; matrix products, arithmetic and copies ran while one was open for 10% -> 11% of each run, Pallas kernels for 15% -> 24%
where the time goes in v2:
time: 271 us
  waiting for transfers between devices  137 us (51%)
  Pallas kernels  65.2 us (24%)
  matrix products  23.6 us (9%)
  between operations  18.2 us (7%)
  local copies, waits for them, and re-layouts  15.1 us (6%)
  other arithmetic  6.63 us (2%)
  starting transfers between devices  5.23 us (2%)
    all_gather x1, waiting for transfers between devices, shards(): first = lax.all_gather(first, 'req', axis=0, tiled=True)  118 us
    pallas_call x4, Pallas kernels, attention(): pl.pallas_call(functools.partial(attention_kernel, per_group, ratio), out...  65.2 us
    dot_general x3, matrix products, shards(): jnp.dot(attn[head], out_weight[head * chunk:(head + 1) * chunk], preferre...  16.1 us
    ppermute x4, waiting for transfers between devices, send(): lax.ppermute(array, 'tp', [(i, (i + shift) % sides) for i in range(sides)])  11.7 us
    all_gather x1, waiting for transfers between devices, shards(): sources.append((lax.all_gather(last_pair, 'req', axis=0, tiled=True), 0))  6.84 us
    unnamed x31, local copies, waits for them, and re-layouts  6.66 us
  transfers between devices with their start and end apart: 6, of which 5 were waited for; matrix products, arithmetic and copies ran while one was open for 11% of the time, Pallas kernels for 24%

profile of v2, /device:TPU:0, one launch (start us, length us, event | category | flops | bytes accessed | tf_op | source)
XLA Modules:
  0.0 270.7 jit_solution(785506269695865663)
XLA Ops:
  7.2 0.0 all-gather.3.cloned.1.call-start
  7.2 1.0 slice_dynamic-update-slice_fusion.5
  8.2 0.0 copy-start.10
  8.3 1.1 slice_dynamic-update-slice_fusion.4
  9.3 1.1 fusion.21
  10.5 1.1 fusion.22
  11.6 1.0 slice_dynamic-update-slice_fusion.1
  12.6 1.0 slice_dynamic-update-slice_fusion
  13.6 1.2 copy-done.3
  14.8 0.0 all-gather.3.cloned.1.call-update
  14.8 0.0 all-gather.5.cloned.1.call-start
  14.9 0.6 dynamic_slice.28
  17.4 0.6 fusion.24
  19.4 0.6 dynamic_slice.31
  19.9 0.2 reshape.36
  20.8 0.1 dynamic_slice.30
  20.9 1.2 pad_add_fusion.numbers
  22.1 0.6 iota_compare_fusion
  22.8 0.5 multiply_cosine_fusion
  23.3 0.1 pad_maximum_fusion.1
  23.5 0.9 pad_maximum_fusion
  24.3 0.3 fusion.23
  24.7 0.4 maximum_multiply_fusion
  25.0 0.1 mul.97
  25.1 0.8 fusion.18.key
  26.0 2.1 constant_dynamic-slice_fusion.1
  28.1 118.2 %all-gather.3.cloned.1.call-done.block = bf16[16,1024,768]{2,1,0:T(8,128)(2,1)} async-done(((bf16[1,1024,768]{2,1,0:T(8,128)(2,1)}), bf16[16,1024,768]{2,1,0:T(8,128)(2,1)}) %all-gather.3.cloned.1.call-update) | async-done | bytes 25165840 | tf_op jit(solution)/shard_map/all_gather | solution.py:183
  146.3 0.0 all-gather.5.cloned.1.call-update
  146.3 1.5 collective-permute-start.2
  147.9 16.4 %shard_map.141 = bf16[256,640]{1,0:T(8,128)(2,1)} custom-call(s32[5]{0:T(128)} %pad_add_fusion.numbers, bf16[256,2560]{1,0:T(8,128)(2,1)} %query.7, bf16[256,512]{1,0:T(8,128)(2,1)} %fusion.18.key, bf16[256,512]{1,0:T(8,128)(2,1)} %value.7, f32[256,128]{1,0:T(8,128)} %copy-done.7, f32[256,128]{1,0:T(8,128)} %copy-done.8, ...), custom_call_target="tpu_custom_call" | custom-call | flops 10737418240 | bytes 2752512 | tf_op jit(solution)/shard_map/pallas_call | solution.py:88
  164.3 16.3 %shard_map.140 = bf16[256,640]{1,0:T(8,128)(2,1)} custom-call(s32[5]{0:T(128)} %pad_add_fusion.numbers, bf16[256,2560]{1,0:T(8,128)(2,1)} %query.7, bf16[256,512]{1,0:T(8,128)(2,1)} %fusion.18.key, bf16[256,512]{1,0:T(8,128)(2,1)} %value.7, f32[256,128]{1,0:T(8,128)} %copy-done.7, f32[256,128]{1,0:T(8,128)} %copy-done.8, ...), custom_call_target="tpu_custom_call" | custom-call | flops 10737418240 | bytes 2752512 | tf_op jit(solution)/shard_map/pallas_call | solution.py:88
  180.6 16.3 %shard_map.139 = bf16[256,640]{1,0:T(8,128)(2,1)} custom-call(s32[5]{0:T(128)} %pad_add_fusion.numbers, bf16[256,2560]{1,0:T(8,128)(2,1)} %query.7, bf16[256,512]{1,0:T(8,128)(2,1)} %fusion.18.key, bf16[256,512]{1,0:T(8,128)(2,1)} %value.7, f32[256,128]{1,0:T(8,128)} %copy-done.7, f32[256,128]{1,0:T(8,128)} %copy-done.8, ...), custom_call_target="tpu_custom_call" | custom-call | flops 10737418240 | bytes 2752512 | tf_op jit(solution)/shard_map/pallas_call | solution.py:88
  196.8 5.3 %fusion.10 = f32[256,5120]{1,0:T(8,128)S(1)} fusion(bf16[256,640]{1,0:T(8,128)(2,1)} %shard_map.139, bf16[2560,5120]{1,0:T(8,128)(2,1)} %param.18), kind=kOutput, calls=%fused_computation.6 | convolution fusion | flops 1677721600 | bytes 12124160 | tf_op jit(solution)/shard_map/dot_general | solution.py:203
  202.1 5.3 %fusion.7 = f32[256,5120]{1,0:T(8,128)S(1)} fusion(f32[256,5120]{1,0:T(8,128)S(1)} %fusion.10, bf16[256,640]{1,0:T(8,128)(2,1)S(1)} %copy-done.6, bf16[2560,5120]{1,0:T(8,128)(2,1)} %param.18), kind=kOutput, calls=%fused_computation.5 | convolution fusion | flops 1679032320 | bytes 17367040 | tf_op jit(solution)/shard_map/dot_general | solution.py:203
  207.4 5.5 %fusion.2 = f32[256,5120]{1,0:T(8,128)S(1)} fusion(f32[256,5120]{1,0:T(8,128)S(1)} %fusion.7, bf16[256,640]{1,0:T(8,128)(2,1)S(1)} %copy-done.5, bf16[2560,5120]{1,0:T(8,128)(2,1)} %param.18), kind=kOutput, calls=%fused_computation.2 | convolution fusion | flops 1679032320 | bytes 17367040 | tf_op jit(solution)/shard_map/dot_general | solution.py:203
  213.0 2.3 copy-done
  215.3 1.2 dynamic-slice_convert_fusion
  216.5 0.6 collective-permute-start
  217.1 6.8 %all-gather.5.cloned.1.call-done.block = bf16[16,1024,256]{2,1,0:T(8,128)(2,1)} async-done(((bf16[1,1024,256]{2,1,0:T(8,128)(2,1)}), bf16[16,1024,256]{2,1,0:T(8,128)(2,1)}) %all-gather.5.cloned.1.call-update) | async-done | bytes 8388624 | tf_op jit(solution)/shard_map/all_gather | solution.py:188
  223.9 16.2 %shard_map.142 = bf16[256,640]{1,0:T(8,128)(2,1)} custom-call(s32[5]{0:T(128)} %pad_add_fusion.numbers, bf16[256,2560]{1,0:T(8,128)(2,1)} %query.7, bf16[256,512]{1,0:T(8,128)(2,1)} %fusion.18.key, bf16[256,512]{1,0:T(8,128)(2,1)} %value.7, f32[256,128]{1,0:T(8,128)} %copy-done.7, f32[256,128]{1,0:T(8,128)} %copy-done.8, ...), custom_call_target="tpu_custom_call" | custom-call | flops 10737418240 | bytes 2752512 | tf_op jit(solution)/shard_map/pallas_call | solution.py:88
  240.2 1.5 collective-permute-start.1
  241.7 3.3 %fusion.12 = f32[256,2560]{1,0:T(8,128)S(1)} fusion(bf16[256,640]{1,0:T(8,128)(2,1)} %shard_map.142, bf16[2560,5120]{1,0:T(8,128)(2,1)} %param.18, s32[]{:T(128)S(6)} %select_n.24), kind=kOutput, calls=%fused_computation.8 | convolution fusion | flops 838860800 | bytes 6225924 | tf_op jit(solution)/shard_map/dot_general | solution.py:215
  245.0 3.4 %collective-permute-done = bf16[256,2560]{1,0:T(8,128)(2,1)} collective-permute-done((bf16[256,2560]{1,0:T(8,128)(2,1)}, bf16[256,2560]{1,0:T(8,128)(2,1)}, u32[]{:S(2)}, u32[]{:S(2)}) %collective-permute-start) | collective-permute-done | bytes 1310752 | tf_op jit(solution)/shard_map/ppermute | solution.py:147
  248.5 6.2 %collective-permute-done.1 = bf16[256,640]{1,0:T(8,128)(2,1)} collective-permute-done((bf16[256,640]{1,0:T(8,128)(2,1)}, bf16[256,640]{1,0:T(8,128)(2,1)}, u32[]{:S(2)}, u32[]{:S(2)}) %collective-permute-start.1) | collective-permute-done | bytes 327712 | tf_op jit(solution)/shard_map/ppermute | solution.py:147
  254.7 4.1 %fusion.14 = (f32[256]{0:T(256)S(1)}, bf16[256,2560]{1,0:T(8,128)(2,1)S(1)}) fusion(f32[256,2560]{1,0:T(8,128)S(1)} %fusion.12, bf16[256,2560]{1,0:T(8,128)(2,1)} %collective-permute-done, f32[256,5120]{1,0:T(8,128)S(1)} %copy-done.1, s32[]{:T(128)S(6)} %select_n.24, bf16[256,5120]{1,0:T(8,128)(2,1)} %param.17, ...), kind=kOutput, calls=%fused_computation.12 | convolution fusion | flops 845414144 | bytes 12780548 | tf_op jit(solution)/shard_map/dot_general | solution.py:217
  258.8 1.5 collective-permute-start.3
  260.3 2.1 collective-permute-done.3
  262.4 1.4 fusion.16
  (30 shorter events, 0.1 us)
Async XLA Ops:
  7.2 139.1 %all-gather.3.cloned.1.call-start = ((), (), s32[]{:S(2)}) async-start(), calls=%async_computation | async-start | bytes 26738688 | tf_op jit(solution)/shard_map/all_gather | solution.py:183
  8.2 6.7 %copy-start.10 = (s32[16]{0:T(128)S(1)}, s32[16]{0:T(128)}, u32[]{:S(2)}) copy-start(s32[16]{0:T(128)} %param.21) | copy-start | bytes 196
  8.2 9.2 %copy-start.11 = (s32[16,1]{0,1:T(1,128)S(1)}, s32[16,1]{0,1:T(1,128)}, u32[]{:S(2)}) copy-start(s32[16,1]{0,1:T(1,128)} %param.23) | copy-start | bytes 196
  8.2 11.1 %copy-start.12 = (s32[16]{0:T(128)S(1)}, s32[16]{0:T(128)}, u32[]{:S(2)}) copy-start(s32[16]{0:T(128)} %param.20) | copy-start | bytes 196
  8.2 11.7 %copy-start.4 = (bf16[256,512]{1,0:T(8,128)(2,1)S(1)}, bf16[256,512]{1,0:T(8,128)(2,1)}, u32[]{:S(2)}) copy-start(bf16[256,512]{1,0:T(8,128)(2,1)} %param.13) | copy-start | bytes 786436
  9.3 11.4 %copy-start.13 = (s32[16]{0:T(128)S(1)}, s32[16]{0:T(128)}, u32[]{:S(2)}) copy-start(s32[16]{0:T(128)} %param.22) | copy-start | bytes 196
  13.6 1.2 copy-start.3
  14.8 209.1 %all-gather.5.cloned.1.call-start = ((), (), s32[]{:S(2)}) async-start(), calls=%async_computation.1 | async-start | bytes 8912896 | tf_op jit(solution)/shard_map/all_gather | solution.py:188
  23.4 1.7 copy-start.7
  23.5 1.7 copy-start.8
  146.3 102.2 %collective-permute-start.2 = (bf16[640,2560]{1,0:T(8,128)(2,1)S(1)}, bf16[640,2560]{1,0:T(8,128)(2,1)}, u32[]{:S(2)}, u32[]{:S(2)}) collective-permute-start(bf16[640,2560]{1,0:T(8,128)(2,1)S(1)} %constant_dynamic-slice_fusion.1), channel_id=1, source_target_pairs={{0,1},{1,0},{2,3},{3,2},{4,5},{5,4},{6,7},{7,6},{8,9},{9,8},{10,11... | collective-permute-start | bytes 9830408 | tf_op jit(solution)/shard_map/ppermute | solution.py:147
  196.8 5.3 %copy-start.6 = (bf16[256,640]{1,0:T(8,128)(2,1)S(1)}, bf16[256,640]{1,0:T(8,128)(2,1)}, u32[]{:S(2)}) copy-start(bf16[256,640]{1,0:T(8,128)(2,1)} %shard_map.140) | copy-start | bytes 983044
  202.1 5.3 %copy-start.5 = (bf16[256,640]{1,0:T(8,128)(2,1)S(1)}, bf16[256,640]{1,0:T(8,128)(2,1)}, u32[]{:S(2)}) copy-start(bf16[256,640]{1,0:T(8,128)(2,1)} %shard_map.141) | copy-start | bytes 983044
  213.0 2.3 copy-start
  216.5 32.0 %collective-permute-start = (bf16[256,2560]{1,0:T(8,128)(2,1)}, bf16[256,2560]{1,0:T(8,128)(2,1)}, u32[]{:S(2)}, u32[]{:S(2)}) collective-permute-start(bf16[256,2560]{1,0:T(8,128)(2,1)} %dynamic-slice_convert_fusion), channel_id=1, source_target_pairs={{0,1},{1,0},{2,3},{3,2},{4,5},{5,4},{6,7},{7,6},{8,9},{9,8},{10,11... | collective-permute-start | bytes 3932168 | tf_op jit(solution)/shard_map/ppermute | solution.py:147
  240.2 14.5 %collective-permute-start.1 = (bf16[256,640]{1,0:T(8,128)(2,1)}, bf16[256,640]{1,0:T(8,128)(2,1)}, u32[]{:S(2)}, u32[]{:S(2)}) collective-permute-start(bf16[256,640]{1,0:T(8,128)(2,1)} %shard_map.142), channel_id=1, source_target_pairs={{0,1},{1,0},{2,3},{3,2},{4,5},{5,4},{6,7},{7,6},{8,9},{9,8},{10,11... | collective-permute-start | bytes 983048 | tf_op jit(solution)/shard_map/ppermute | solution.py:147
  241.7 13.0 %copy-start.1 = (f32[256,5120]{1,0:T(8,128)S(1)}, f32[256,5120]{1,0:T(8,128)}, u32[]{:S(2)}) copy-start(f32[256,5120]{1,0:T(8,128)} %copy-done) | copy-start | bytes 15728644
  245.0 15.3 %copy-start.9 = (bf16[2560]{0:T(1024)(128)(2,1)S(1)}, bf16[2560]{0:T(1024)(128)(2,1)}, u32[]{:S(2)}) copy-start(bf16[2560]{0:T(1024)(128)(2,1)} %param.19) | copy-start | bytes 15364
  258.8 5.1 %copy-start.2 = (bf16[256,2560]{1,0:T(8,128)(2,1)}, bf16[256,2560]{1,0:T(8,128)(2,1)S(1)}, u32[]{:S(2)}) copy-start(bf16[256,2560]{1,0:T(8,128)(2,1)S(1)} %get-tuple-element.18) | copy-start | bytes 3932164
  258.8 3.6 %collective-permute-start.3 = (f32[256]{0:T(256)S(1)}, f32[256]{0:T(256)S(1)}, u32[]{:S(2)}, u32[]{:S(2)}) collective-permute-start(f32[256]{0:T(256)S(1)} %get-tuple-element.17), channel_id=1, source_target_pairs={{0,1},{1,0},{2,3},{3,2},{4,5},{5,4},{6,7},{7,6},{8,9},{9,8},{10,11... | collective-permute-start | bytes 3080 | tf_op jit(solution)/shard_map/ppermute | solution.py:147
Sparse Core Ops, SparseCore 0:
  15.0 131.2 all-gather.2
  149.0 74.8 all-gather.4
